TPU v7x, 32 devices: a whole 2x2x4 slice. The times are simulated.
32 devices in a mesh: replica: 8 (over y, x, core), fsdp: 4 (over z).
Axes of the slice: x: 2, y: 2, z: 4, core: 2. Of those that a mesh axis runs over, the one named last changes fastest.
Arguments:
- activations: bfloat16 [8, 1792, 4096], P('replica', 'fsdp'), may hold values from -84 to 84
- targets: bfloat16 [8, 1792, 512], P('replica', 'fsdp'), may hold values from -8 to 8
- weights: float32 [8, 4096, 512], P('replica', 'fsdp'), may hold values from -19 to 19
- lengths: int32 [8, 28], P('replica'), may hold values from 1 to 64, 896 in all within a row
Outputs:
- averaged: float32 [8, 4096, 512], P('replica', 'fsdp')
Inputs may be any that keep to these rules, and one draw needn't show every extreme that they name: `lengths`: each row sums to 896; sequence s of a replica fills slot s from its first position.
All inputs are finite; a program needn't handle non-finite values.
Results may differ from a plain program's by a relative error of at most 0.0014.
Values may be sent and summed in bfloat16 or wider, within the bound.
No kernel may reach another device: no remote copies, remote signals or barrier semaphores. Data moves between devices by JAX's collectives and lax.ppermute only.
A program may use at most 64 MiB of HBM per device.

v0:
```python
import functools

import jax
import jax.numpy as jnp
from jax import lax
from jax.experimental import pallas as pl
from jax.experimental.pallas import tpu as pltpu
from jax.sharding import PartitionSpec as P

SLOT = 64
STEP = 3
ALIGN = 16
HALVES = 2

learning_rate = 0.1
epsilon = 1e-06


def swapped(value, axis, bit):
    mask = 2**bit
    pairs = [(source, source ^ mask) for source in range(lax.axis_size(axis))]
    return lax.ppermute(value, axis, pairs)


def turned(value, distance):
    members = lax.axis_size("fsdp")
    ring = [(source, (source + distance) % members) for source in range(members)]
    return lax.ppermute(value, "fsdp", ring)


def live_before(lengths_ref, members):
    sequences = lengths_ref.shape[1] // members
    totals = [jnp.int32(0)]
    for member in range(members):
        total = totals[-1]
        for q in range(sequences):
            total = total + lengths_ref[0, member * sequences + q]
        totals.append(total)
    return totals


def chosen(values, index):
    value = values[0]
    for i in range(1, len(values)):
        value = jnp.where(index == i, values[i], value)
    return value


def aligned(place):
    return pl.multiple_of(place // ALIGN * ALIGN, ALIGN)


def token_places(lengths_ref, member, before, tokens):
    sequences = tokens // SLOT
    place = before % ALIGN
    slot = lax.broadcasted_iota(jnp.int32, (1, tokens), 1)
    places = jnp.full((1, tokens), -1, jnp.int32)
    for s in range(sequences):
        length = lengths_ref[0, member * sequences + s]
        position = slot - s * SLOT
        places = jnp.where((position >= 0) & (position < length), position + place, places)
        place = place + length
    return places


def picking(places, start, rows):
    row = lax.broadcasted_iota(jnp.int32, (rows, places.shape[1]), 0) + start
    return jnp.where(row == places, 1.0, 0.0).astype(jnp.bfloat16)


class Block:
    def __init__(self, features_ref, member, block_ref, sems):
        self.block_ref, self.width = block_ref, block_ref.shape[1] // sems.shape[0]
        start = member * block_ref.shape[1]
        self.copies = []
        for j in range(sems.shape[0]):
            there = pl.ds(pl.multiple_of(start + j * self.width, 128), self.width)
            here = pl.ds(j * self.width, self.width)
            copy = pltpu.make_async_copy(
                features_ref.at[:, there], block_ref.at[:, here], sems.at[j]
            )
            copy.start()
            self.copies.append(copy)

    def picked(self, pick, store, wait):
        for j, copy in enumerate(self.copies):
            if wait:
                copy.wait()
            here = slice(j * self.width, (j + 1) * self.width)
            rows = jnp.dot(pick, self.block_ref[:, here], preferred_element_type=jnp.float32)
            store(here, rows.astype(jnp.bfloat16))


def used_places(totals, first, sizes):
    choices = []
    for member in range(len(totals) - 1):
        used = totals[member + 1] - aligned(totals[member])
        choice = jnp.int32(0)
        for size in sizes[:-1]:
            choice = choice + jnp.where(used > first + size, 1, 0)
        choices.append(choice)
    return choices


def choice_bits(sizes):
    return (len(sizes) - 1).bit_length()


def sent_kernel(members, offsets, sizes, lengths_ref, features_ref, *refs):
    count = len(offsets)
    outs, choice_ref = refs[: 2 * count], refs[2 * count]
    block_ref, first_ref, more_ref, sems, out_sems, more_sems = refs[2 * count + 1 :]
    index = lax.axis_index("fsdp")
    blocks = [
        Block(features_ref, lax.rem(index + i, members), block_ref.at[n], sems.at[n])
        for n, i in enumerate(offsets)
    ]
    totals = live_before(lengths_ref, members)
    before, end = chosen(totals[:-1], index), chosen(totals[1:], index)
    places = token_places(lengths_ref, index, before, block_ref.shape[1])
    first, more = first_ref.shape[1], more_ref.shape[1]
    pick = picking(places, 0, first)
    copies = []
    for n, block in enumerate(blocks):

        def store(here, rows, n=n):
            first_ref[n, :, here] = rows
            copy = pltpu.make_async_copy(
                first_ref.at[n, :, here],
                outs[n].at[:, here],
                out_sems.at[n, here.start // (here.stop - here.start)],
            )
            copy.start()
            copies.append(copy)

        block.picked(pick, store, True)

    @pl.when(end - aligned(before) > first)
    def _():
        further = picking(places, first, more)
        for n, block in enumerate(blocks):

            def store(here, rows, n=n):
                more_ref[n, :, here] = rows

            block.picked(further, store, False)
            copy = pltpu.make_async_copy(more_ref.at[n], outs[count + n], more_sems.at[n])
            copy.start()
            copy.wait()

    packed = jnp.int32(0)
    for member, choice in enumerate(used_places(totals, first, sizes)):
        packed = packed | (choice << (member * choice_bits(sizes)))
    choice_ref[0] = packed
    for copy in copies:
        copy.wait()


def own_kernel(
    members,
    far,
    scale,
    lengths_ref,
    features_ref,
    targets_ref,
    master_ref,
    partner_ref,
    far_ref,
    *refs,
):
    held_more = refs[:members]
    rows_ref, keys_ref, low_ref, halves_ref = refs[members : members + 4]
    block_ref, first_ref, more_ref, sems, first_sem, more_sems = refs[members + 4 :]
    index = lax.axis_index("fsdp")
    block = Block(features_ref, index, block_ref, sems)
    far_copy = pltpu.make_async_copy(far_ref, first_ref, first_sem)
    far_copy.start()
    rows_ref[...] = jnp.zeros_like(rows_ref)
    low_ref[...] = master_ref[...].astype(jnp.bfloat16)
    halves_ref[...] = 0.5 * (master_ref[...] + partner_ref[...])
    totals = live_before(lengths_ref, members)
    before = chosen(totals[:-1], index)
    first, more = first_ref.shape[0], more_ref.shape[0]
    places = token_places(lengths_ref, index, before, block_ref.shape[0])
    pick = picking(places, 0, first + more)

    def store(here, rows):
        rows_ref[pl.ds(aligned(before), first + more), here] = rows

    block.picked(pick, store, True)
    far_start = aligned(chosen(totals[:-1], lax.rem(index + members - far, members)))
    far_copy.wait()
    rows_ref[pl.ds(far_start, first)] += first_ref[...]
    for member in range(members):
        start = aligned(totals[member])
        used = totals[member + 1] - start

        @pl.when((member != index) & (used > first))
        def _(member=member, start=start, used=used):
            copy = pltpu.make_async_copy(held_more[member], more_ref, more_sems.at[member])
            copy.start()
            copy.wait()
            for k in range(0, more, ALIGN):

                @pl.when(used > first + k)
                def _(k=k):
                    rows_ref[pl.ds(start + first + k, ALIGN)] += more_ref[k : k + ALIGN]

    height = (rows_ref.shape[0] - first - more) // members

    @pl.loop(0, members)
    def _(j):
        here = pl.ds(pl.multiple_of(j * height, ALIGN), height)
        keys_ref[here] = (
            jnp.dot(rows_ref[here], low_ref[...], preferred_element_type=jnp.float32) * scale
        )

    keys_ref[pl.ds(aligned(before), first + more)] -= jnp.dot(
        pick, targets_ref[...], preferred_element_type=jnp.float32
    )


def keys_kernel(members, near, scale, lengths_ref, low_ref, keys_ref, *refs):
    blocks, sums, total_ref = refs[: len(near)], refs[len(near) : -1], refs[-1]
    share, width = sums[0].shape

    @pl.loop(0, members)
    def _(j):
        rows = pl.ds(pl.multiple_of(j * share, ALIGN), share)
        total_ref[rows] = keys_ref[rows]

    index = lax.axis_index("fsdp")
    totals = live_before(lengths_ref, members)
    for i, block_ref in zip(near, blocks):
        start = aligned(chosen(totals[:-1], lax.rem(index + members - i, members)))
        total_ref[pl.ds(start, block_ref.shape[0])] += (
            jnp.dot(block_ref[...], low_ref[...], preferred_element_type=jnp.float32) * scale
        )
    for half in range(HALVES):
        for i in range(members):
            owner = lax.rem(index + i, members)
            rows = pl.ds(pl.multiple_of(owner * share, ALIGN), share)
            out_ref = sums[half * members + i]
            here = slice(half * width, (half + 1) * width)
            out_ref[...] = total_ref[rows, here].astype(out_ref.dtype)


def turn_kernel(members, near, lengths_ref, rows_ref, *refs):
    blocks, (turned_ref, all_ref) = refs[: len(near)], refs[len(near) :]
    index = lax.axis_index("fsdp")
    totals = live_before(lengths_ref, members)
    all_ref[...] = rows_ref[...]
    for i, block_ref in zip(near, blocks):
        start = aligned(chosen(totals[:-1], lax.rem(index + members - i, members)))
        all_ref[pl.ds(start, block_ref.shape[0])] += block_ref[...]
    for start in range(0, turned_ref.shape[1], 128):
        turned_ref[:, start : start + 128] = all_ref[start : start + 128, :].T


def gradient_kernel(members, turned_ref, *refs):
    residuals, (gradient_ref, low_ref, squares_ref, all_ref) = refs[:members], refs[members:]
    index = lax.axis_index("fsdp")
    share = residuals[0].shape[0]
    for i in range(members):
        owner = lax.rem(index + members - i, members)
        all_ref[pl.ds(pl.multiple_of(owner * share, ALIGN), share)] = residuals[i][...]
    squares_ref[...] = jnp.zeros_like(squares_ref)
    height = min(256, turned_ref.shape[0])

    @pl.loop(0, turned_ref.shape[0] // height)
    def _(j):
        rows = pl.ds(pl.multiple_of(j * height, height), height)
        gradient = jnp.dot(turned_ref[rows], all_ref[...], preferred_element_type=jnp.float32)
        gradient_ref[rows] = gradient
        low_ref[rows] = gradient.astype(low_ref.dtype)
        squares = jnp.sum((gradient * gradient).reshape(-1, 8, gradient.shape[1]), axis=0)
        lanes = squares.shape[1] // 128
        squares_ref[...] += sum(squares[:, 128 * k : 128 * (k + 1)] for k in range(lanes))


def average_kernel(entries, own_ref, other_ref, halves_ref, *refs):
    gradients, partners, (out_ref, done_ref, sems) = refs[:HALVES], refs[HALVES:-3], refs[-3:]
    rate = 0.5 * learning_rate
    own = rate * lax.rsqrt(jnp.sum(own_ref[...], keepdims=True) / entries + epsilon)
    other = rate * lax.rsqrt(jnp.sum(other_ref[...], keepdims=True) / entries + epsilon)
    pieces = sems.shape[0]
    height = done_ref.shape[0] // pieces
    width = done_ref.shape[1] // HALVES
    copies = []
    for j in range(pieces):
        rows = pl.ds(j * height, height)
        for half in range(HALVES):
            here = slice(half * width, (half + 1) * width)
            done_ref[rows, here] = (
                halves_ref[rows, here]
                - gradients[half][rows] * own
                - partners[half][rows].astype(jnp.float32) * other
            )
        copies.append(pltpu.make_async_copy(done_ref.at[rows], out_ref.at[rows], sems.at[j]))
        copies[-1].start()
    for copy in copies:
        copy.wait()


def more_rows(size, source, offsets, blocks):
    if size == 0:
        return blocks[0]
    members = lax.axis_size("fsdp")
    moved = [
        lax.ppermute(block[:size], "fsdp", [(source, (source + i) % members)])
        for i, block in zip(offsets, blocks)
    ]
    return jnp.pad(sum(moved[1:], moved[0]), ((0, blocks[0].shape[0] - size), (0, 0)))


def local(activations, targets, weights, lengths):
    features = activations[0]
    wanted = targets[0]
    master = weights[0]
    tokens_here = features.shape[0]
    local_rows, columns = master.shape
    members = lax.axis_size("fsdp")
    distance_bit = STEP % (lax.axis_size("replica").bit_length() - 1)
    share = tokens_here // 2
    first = -(-(share + 32) // ALIGN) * ALIGN
    more = -(-(tokens_here + ALIGN - first) // ALIGN) * ALIGN
    steps = (16, 32, 48, 64, 80, 96, 128) if members <= 4 else (96,)
    sizes = [0] + [size for size in steps if size < more] + [more]
    most = first + more
    scale = features.shape[1] ** (-0.5)
    places = members * share + most

    vmem = pl.BlockSpec(memory_space=pltpu.VMEM)
    anywhere = pl.BlockSpec(memory_space=pl.ANY)
    smem = pl.BlockSpec(memory_space=pltpu.SMEM)
    params = pltpu.CompilerParams(vmem_limit_bytes=16 * 2**20)
    middle = pltpu.CompilerParams(vmem_limit_bytes=24 * 2**20)
    large = pltpu.CompilerParams(vmem_limit_bytes=56 * 2**20)

    def array(rows, width, dtype):
        return jax.ShapeDtypeStruct((rows, width), dtype)

    def cost(flops, moved):
        return pl.CostEstimate(flops=flops, bytes_accessed=moved, transcendentals=0)

    def sent_to(offsets):
        count = len(offsets)
        pieces = max(1, local_rows // 256)
        *arrays, choice = pl.pallas_call(
            functools.partial(sent_kernel, members, offsets, sizes),
            in_specs=[smem, anywhere],
            out_specs=[anywhere] * (2 * count) + [smem],
            out_shape=[
                array(rows, local_rows, jnp.bfloat16) for rows in (first, more) for _ in offsets
            ]
            + [jax.ShapeDtypeStruct((1,), jnp.int32)],
            scratch_shapes=[
                pltpu.VMEM((count, tokens_here, local_rows), jnp.bfloat16),
                pltpu.VMEM((count, first, local_rows), jnp.bfloat16),
                pltpu.VMEM((count, more, local_rows), jnp.bfloat16),
                pltpu.SemaphoreType.DMA((count, pieces)),
                pltpu.SemaphoreType.DMA((count, pieces)),
                pltpu.SemaphoreType.DMA((count,)),
            ],
            compiler_params=large,
            cost_estimate=cost(
                2 * count * first * tokens_here * local_rows,
                2 * count * (tokens_here + first) * local_rows,
            ),
        )(lengths, features)
        return arrays[:count], arrays[count:], choice

    far = members // 2
    near = [i for i in range(1, members) if i != far]
    far_first, far_more, choice = sent_to([far])
    near_first, near_more, _ = sent_to(near)
    held_far = turned(far_first[0], far)
    offsets = [far] + near
    bits = choice_bits(sizes)
    held_more = [
        lax.switch(
            lax.shift_right_logical(choice[0], jnp.int32(source * bits)) & (2**bits - 1),
            [functools.partial(more_rows, size, source, offsets) for size in sizes],
            far_more + near_more,
        )
        for source in range(members)
    ]
    near_first, held_more, late_lengths = lax.optimization_barrier((near_first, held_more, lengths))
    held = [turned(block, i) for i, block in zip(near, near_first)]

    partner_master = swapped(master, "replica", distance_bit)
    rows, keys, low, halves = pl.pallas_call(
        functools.partial(own_kernel, members, far, scale),
        in_specs=[smem, anywhere, vmem, vmem, vmem, anywhere] + [anywhere] * members,
        out_specs=[vmem] * 4,
        out_shape=[
            array(places, local_rows, jnp.bfloat16),
            array(places, columns, jnp.float32),
            array(local_rows, columns, jnp.bfloat16),
            array(local_rows, columns, jnp.float32),
        ],
        scratch_shapes=[
            pltpu.VMEM((tokens_here, local_rows), jnp.bfloat16),
            pltpu.VMEM((first, local_rows), jnp.bfloat16),
            pltpu.VMEM((more, local_rows), jnp.bfloat16),
            pltpu.SemaphoreType.DMA((max(1, local_rows // 256),)),
            pltpu.SemaphoreType.DMA,
            pltpu.SemaphoreType.DMA((members,)),
        ],
        compiler_params=middle,
        cost_estimate=cost(
            2 * (most * tokens_here + members * share * columns) * (local_rows + columns),
            20 * local_rows * columns,
        ),
    )(late_lengths, features, wanted, master, partner_master, held_far, *held_more)

    width = columns // HALVES
    sum_shapes = [array(share, width, jnp.bfloat16 if i else jnp.float32) for i in range(members)]
    *sums, _ = pl.pallas_call(
        functools.partial(keys_kernel, members, near, scale),
        in_specs=[smem, vmem, vmem] + [vmem] * len(near),
        out_specs=[vmem] * (HALVES * members + 1),
        out_shape=sum_shapes * HALVES + [array(places, columns, jnp.float32)],
        input_output_aliases={2: HALVES * members},
        compiler_params=params,
        cost_estimate=cost(
            2 * len(near) * first * local_rows * columns, 8 * places * columns
        ),
    )(lengths, low, keys, *held)
    sums = [sums[half * members : (half + 1) * members] for half in range(HALVES)]

    turned_rows = pl.pallas_call(
        functools.partial(turn_kernel, members, near),
        in_specs=[smem, vmem] + [vmem] * len(near),
        out_specs=vmem,
        out_shape=array(local_rows, members * share, jnp.bfloat16),
        scratch_shapes=[pltpu.VMEM((places, local_rows), jnp.bfloat16)],
        compiler_params=params,
        cost_estimate=cost(0, 4 * members * share * local_rows),
    )(lengths, rows, *held)

    gradients, partners, squares = [], [], 0.0
    for half in range(HALVES):
        residual = sums[half][0]
        for i in range(1, members):
            residual = residual + turned(sums[half][i], i).astype(jnp.float32)
        residual = residual.astype(jnp.bfloat16)
        residuals = [residual] + [turned(residual, i) for i in range(1, members)]
        gradient, low_gradient, own_squares = pl.pallas_call(
            functools.partial(gradient_kernel, members),
            in_specs=[vmem] + [vmem] * members,
            out_specs=[vmem] * 3,
            out_shape=[
                array(local_rows, width, jnp.float32),
                array(local_rows, width, jnp.bfloat16),
                array(8, 128, jnp.float32),
            ],
            scratch_shapes=[pltpu.VMEM((members * share, width), jnp.bfloat16)],
            compiler_params=params,
            cost_estimate=cost(
                2 * members * share * local_rows * width, 8 * local_rows * width
            ),
        )(turned_rows, *residuals)
        gradients.append(gradient)
        partners.append(swapped(low_gradient, "replica", distance_bit))
        squares = squares + own_squares

    total = squares
    for i in range(1, members):
        total = total + turned(squares, i)
    partner_total = swapped(total, "replica", distance_bit)

    averaged = pl.pallas_call(
        functools.partial(average_kernel, members * local_rows * columns),
        in_specs=[vmem] * (3 + 2 * HALVES),
        out_specs=anywhere,
        out_shape=array(local_rows, columns, jnp.float32),
        scratch_shapes=[
            pltpu.VMEM((local_rows, columns), jnp.float32),
            pltpu.SemaphoreType.DMA((4,)),
        ],
        compiler_params=params,
    )(total, partner_total, halves, *gradients, *partners)
    return averaged[None]


def solution(mesh):
    return jax.shard_map(
        local,
        mesh=mesh,
        in_specs=(
            P("replica", "fsdp", None),
            P("replica", "fsdp", None),
            P("replica", "fsdp", None),
            P("replica", None),
        ),
        out_specs=P("replica", "fsdp", None),
        check_vma=False,
    )
```

profile of v0, /device:TPU:7, one launch (start us, length us, event | category | flops | bytes accessed | tf_op | source)
XLA Modules:
  0.0 114.0 jit_solution(16661359957725729006)
XLA Ops:
  0.7 4.0 %shard_map.47 = (bf16[256,1024]{1,0:T(8,128)(2,1)}, bf16[208,1024]{1,0:T(8,128)(2,1)S(1)}, s32[1]{0:T(128)}) custom-call(s32[1,28]{1,0:T(1,128)} %lengths_ref.8, bf16[448,4096]{1,0:T(8,128)(2,1)} %bitcast.8), custom_call_target="tpu_custom_call" | custom-call | flops 234881024 | bytes 1441792 | tf_op jit(solution)/shard_map/pallas_call | solution.py:349
  4.7 2.4 %collective-permute-start.97 = (bf16[256,1024]{1,0:T(8,128)(2,1)}, bf16[256,1024]{1,0:T(8,128)(2,1)S(1)}, u32[]{:S(2)}, u32[]{:S(2)}) collective-permute-start(bf16[256,1024]{1,0:T(8,128)(2,1)} %get-tuple-element.376), channel_id=1, source_target_pairs={{0,2},{1,3},{2,0},{3,1},{4,6},{5,7},{6,4},{7,5},{8,10},{9,11},{10,... | collective-permute-start | bytes 1572872 | tf_op jit(solution)/shard_map/ppermute | solution.py:28
  9.6 5.3 %shard_map.46 = (bf16[256,1024]{1,0:T(8,128)(2,1)}, bf16[256,1024]{1,0:T(8,128)(2,1)}, bf16[208,1024]{1,0:T(8,128)(2,1)S(1)}, bf16[208,1024]{1,0:T(8,128)(2,1)S(1)}, s32[1]{0:T(128)}) custom-call(s32[1,28]{1,0:T(1,128)} %lengths_ref.8, bf16[448,4096]{1,0:T(8,128)(2,1)} %bitcast.9), custom_call_target="tpu_custom_call" | custom-call | flops 469762048 | bytes 2883584 | tf_op jit(solution)/shard_map/pallas_call | solution.py:349
  15.0 0.9 copy-done.6
  16.7 15.0 %conditional.5 = (bf16[208,1024]{1,0:T(8,128)(2,1)S(1)}) conditional(s32[]{:T(128)} %bitcast.2, bf16[208,1024]{1,0:T(8,128)(2,1)S(1)} %get-tuple-element.372, (bf16[208,1024]{1,0:T(8,128)(2,1)S(1)}, bf16[208,1024]{1,0:T(8,128)(2,1)S(1)}, bf16[208,1024]{1,0:T(8,128)(2,1)S(1)}) %tuple.114, ...), branch_computations={%region_9.10_spmd, %region_10.11_spmd, %region_11.12_spmd, %region... | conditional | flops 425984 | bytes 6815872 | solution.py:381
  16.7 1.3 %collective-permute-start.26 = (bf16[16,1024]{1,0:T(8,128)(2,1)S(1)}, bf16[16,1024]{1,0:T(8,128)(2,1)S(1)}, u32[]{:S(2)}, u32[]{:S(2)}) collective-permute-start(bf16[16,1024]{1,0:T(8,128)(2,1)S(1)} %slice.191), channel_id=1, source_target_pairs={{1,0},{5,4},{9,8},{13,12},{17,16},{21,20},{25,24},{29,28}} | collective-permute-start | bytes 98312 | tf_op jit(solution)/shard_map/cond/branch_1_fun/ppermute | solution.py:310
  19.4 12.3 %collective-permute-done.26 = bf16[16,1024]{1,0:T(8,128)(2,1)S(1)} collective-permute-done((bf16[16,1024]{1,0:T(8,128)(2,1)S(1)}, bf16[16,1024]{1,0:T(8,128)(2,1)S(1)}, u32[]{:S(2)}, u32[]{:S(2)}) %collective-permute-start.26) | collective-permute-done | bytes 32800 | tf_op jit(solution)/shard_map/cond/branch_1_fun/ppermute | solution.py:310
  32.5 1.2 %collective-permute-start.98 = (bf16[256,1024]{1,0:T(8,128)(2,1)}, bf16[256,1024]{1,0:T(8,128)(2,1)S(1)}, u32[]{:S(2)}, u32[]{:S(2)}) collective-permute-start(bf16[256,1024]{1,0:T(8,128)(2,1)} %get-tuple-element.382), channel_id=1, source_target_pairs={{0,1},{1,2},{2,3},{3,0},{4,5},{5,6},{6,7},{7,4},{8,9},{9,10},{10,1... | collective-permute-start | bytes 1572872 | tf_op jit(solution)/shard_map/ppermute | solution.py:28
  33.7 2.6 %collective-permute-start.99 = (bf16[256,1024]{1,0:T(8,128)(2,1)}, bf16[256,1024]{1,0:T(8,128)(2,1)S(1)}, u32[]{:S(2)}, u32[]{:S(2)}) collective-permute-start(bf16[256,1024]{1,0:T(8,128)(2,1)} %get-tuple-element.383), channel_id=1, source_target_pairs={{0,3},{1,0},{2,1},{3,2},{4,7},{5,4},{6,5},{7,6},{8,11},{9,8},{10,9... | collective-permute-start | bytes 1572872 | tf_op jit(solution)/shard_map/ppermute | solution.py:28
  36.3 2.0 %copy-done = bf16[1,448,4096]{2,1,0:T(8,128)(2,1)S(1)} copy-done((bf16[1,448,4096]{2,1,0:T(8,128)(2,1)S(1)}, bf16[1,448,4096]{2,1,0:T(8,128)(2,1)}, u32[]{:S(2)}) %copy-start) | copy-done | bytes 3670040
  38.4 7.2 %shard_map.48 = (bf16[1360,1024]{1,0:T(8,128)(2,1)S(1)}, f32[1360,512]{1,0:T(8,128)S(1)}, bf16[1024,512]{1,0:T(8,128)(2,1)S(1)}, f32[1024,512]{1,0:T(8,128)S(1)}) custom-call(s32[1,28]{1,0:T(1,128)S(1)} %copy-done.3, bf16[448,4096]{1,0:T(8,128)(2,1)S(1)} %bitcast.10, bf16[448,512]{1,0:T(8,128)(2,1)S(1)} %bitcast.13, f32[1024,512]{1,0:T(8,128)S(1)} %bitcast.12, ...), custom_call_target="tpu_custom_call" | custom-call | flops 2047868928 | bytes 10485760 | tf_op jit(solution)/shard_map/pallas_call | solution.py:392
  45.9 12.0 %collective-permute-done.99.refs_1_ = bf16[256,1024]{1,0:T(8,128)(2,1)S(1)} collective-permute-done((bf16[256,1024]{1,0:T(8,128)(2,1)}, bf16[256,1024]{1,0:T(8,128)(2,1)S(1)}, u32[]{:S(2)}, u32[]{:S(2)}) %collective-permute-start.99) | collective-permute-done | bytes 524320 | tf_op jit(solution)/shard_map/ppermute | solution.py:28
  57.9 1.6 %shard_map.50 = (f32[224,256]{1,0:T(8,128)S(1)}, bf16[224,256]{1,0:T(8,128)(2,1)S(1)}, bf16[224,256]{1,0:T(8,128)(2,1)S(1)}, bf16[224,256]{1,0:T(8,128)(2,1)S(1)...) custom-call(s32[1,28]{1,0:T(1,128)S(1)} %copy-done.3, ...), custom_call_target="tpu_custom_call", output_to_operand_aliasing={{8}: (2, {})} | custom-call | flops 536870912 | bytes 5570560 | tf_op jit(solution)/shard_map/pallas_call | solution.py:419
  59.5 2.5 %collective-permute-start.106 = (bf16[224,256]{1,0:T(8,128)(2,1)S(1)}, bf16[224,256]{1,0:T(8,128)(2,1)S(1)}, u32[]{:S(2)}, u32[]{:S(2)}) collective-permute-start(bf16[224,256]{1,0:T(8,128)(2,1)S(1)} %get-tuple-element.392), channel_id=1, source_target_pairs={{0,1},{1,2},{2,3},{3,0},{4,5},{5,6},{6,7},{7,4},{8,9},{9,10},{10,1... | collective-permute-start | bytes 344072 | tf_op jit(solution)/shard_map/ppermute | solution.py:28
  62.0 2.2 %collective-permute-start.108 = (bf16[224,256]{1,0:T(8,128)(2,1)S(1)}, bf16[224,256]{1,0:T(8,128)(2,1)S(1)}, u32[]{:S(2)}, u32[]{:S(2)}) collective-permute-start(bf16[224,256]{1,0:T(8,128)(2,1)S(1)} %get-tuple-element.394), channel_id=1, source_target_pairs={{0,3},{1,0},{2,1},{3,2},{4,7},{5,4},{6,5},{7,6},{8,11},{9,8},{10,9... | collective-permute-start | bytes 344072 | tf_op jit(solution)/shard_map/ppermute | solution.py:28
  64.1 1.7 %collective-permute-start.101 = (bf16[224,256]{1,0:T(8,128)(2,1)S(1)}, bf16[224,256]{1,0:T(8,128)(2,1)S(1)}, u32[]{:S(2)}, u32[]{:S(2)}) collective-permute-start(bf16[224,256]{1,0:T(8,128)(2,1)S(1)} %get-tuple-element.388), channel_id=1, source_target_pairs={{0,2},{1,3},{2,0},{3,1},{4,6},{5,7},{6,4},{7,5},{8,10},{9,11},{10,... | collective-permute-start | bytes 344072 | tf_op jit(solution)/shard_map/ppermute | solution.py:28
  65.8 1.6 %collective-permute-start.102 = (bf16[224,256]{1,0:T(8,128)(2,1)S(1)}, bf16[224,256]{1,0:T(8,128)(2,1)S(1)}, u32[]{:S(2)}, u32[]{:S(2)}) collective-permute-start(bf16[224,256]{1,0:T(8,128)(2,1)S(1)} %get-tuple-element.389), channel_id=1, source_target_pairs={{0,3},{1,0},{2,1},{3,2},{4,7},{5,4},{6,5},{7,6},{8,11},{9,8},{10,9... | collective-permute-start | bytes 344072 | tf_op jit(solution)/shard_map/ppermute | solution.py:28
  67.4 5.9 %collective-permute-done.107 = bf16[224,256]{1,0:T(8,128)(2,1)S(1)} collective-permute-done((bf16[224,256]{1,0:T(8,128)(2,1)S(1)}, bf16[224,256]{1,0:T(8,128)(2,1)S(1)}, u32[]{:S(2)}, u32[]{:S(2)}) %collective-permute-start.107) | collective-permute-done | bytes 114720 | tf_op jit(solution)/shard_map/ppermute | solution.py:28
  73.4 7.0 %collective-permute-start.110 = (bf16[224,256]{1,0:T(8,128)(2,1)S(1)}, bf16[224,256]{1,0:T(8,128)(2,1)S(1)}, u32[]{:S(2)}, u32[]{:S(2)}) collective-permute-start(bf16[224,256]{1,0:T(8,128)(2,1)S(1)} %add_convert_fusion.refs_0_), channel_id=1, source_target_pairs={{0,2},{1,3},{2,0},{3,1},{4,6},{5,7},{6,4},{7,5},{8,10},{9,11},{10,... | collective-permute-start | bytes 344072 | tf_op jit(solution)/shard_map/ppermute | solution.py:28
  81.3 6.9 %collective-permute-start.105 = (bf16[224,256]{1,0:T(8,128)(2,1)S(1)}, bf16[224,256]{1,0:T(8,128)(2,1)S(1)}, u32[]{:S(2)}, u32[]{:S(2)}) collective-permute-start(bf16[224,256]{1,0:T(8,128)(2,1)S(1)} %add_convert_fusion.1.refs_0_), channel_id=1, source_target_pairs={{0,3},{1,0},{2,1},{3,2},{4,7},{5,4},{6,5},{7,6},{8,11},{9,8},{10,9... | collective-permute-start | bytes 344072 | tf_op jit(solution)/shard_map/ppermute | solution.py:28
  88.2 2.0 %collective-permute-start.104 = (bf16[224,256]{1,0:T(8,128)(2,1)S(1)}, bf16[224,256]{1,0:T(8,128)(2,1)S(1)}, u32[]{:S(2)}, u32[]{:S(2)}) collective-permute-start(bf16[224,256]{1,0:T(8,128)(2,1)S(1)} %add_convert_fusion.1.refs_0_), channel_id=1, source_target_pairs={{0,2},{1,3},{2,0},{3,1},{4,6},{5,7},{6,4},{7,5},{8,10},{9,11},{10,... | collective-permute-start | bytes 344072 | tf_op jit(solution)/shard_map/ppermute | solution.py:28
  90.2 1.2 %collective-permute-start.103 = (bf16[224,256]{1,0:T(8,128)(2,1)S(1)}, bf16[224,256]{1,0:T(8,128)(2,1)S(1)}, u32[]{:S(2)}, u32[]{:S(2)}) collective-permute-start(bf16[224,256]{1,0:T(8,128)(2,1)S(1)} %add_convert_fusion.1.refs_0_), channel_id=1, source_target_pairs={{0,1},{1,2},{2,3},{3,0},{4,5},{5,6},{6,7},{7,4},{8,9},{9,10},{10,1... | collective-permute-start | bytes 344072 | tf_op jit(solution)/shard_map/ppermute | solution.py:28
  91.4 1.3 %shard_map.49.turned_ref = bf16[1024,896]{1,0:T(8,128)(2,1)S(1)} custom-call(s32[1,28]{1,0:T(1,128)S(1)} %copy-done.3, bf16[1360,1024]{1,0:T(8,128)(2,1)S(1)} %get-tuple-element.381.rows_ref, bf16[256,1024]{1,0:T(8,128)(2,1)S(1)} %collective-permute-done.98.refs_0_, bf16[256,1024]{1,0:T(8,128)(2,1)S(1)} %collective-permute-done.99.refs_1_), custom_call_target="tpu_custom_call" | custom-call | bytes 3670016 | tf_op jit(solution)/shard_map/pallas_call | solution.py:432
  92.7 2.1 %collective-permute-done.110.refs_2_ = bf16[224,256]{1,0:T(8,128)(2,1)S(1)} collective-permute-done((bf16[224,256]{1,0:T(8,128)(2,1)S(1)}, bf16[224,256]{1,0:T(8,128)(2,1)S(1)}, u32[]{:S(2)}, u32[]{:S(2)}) %collective-permute-start.110) | collective-permute-done | bytes 114720 | tf_op jit(solution)/shard_map/ppermute | solution.py:28
  94.9 1.3 %shard_map.52 = (f32[1024,256]{1,0:T(8,128)S(1)}, bf16[1024,256]{1,0:T(8,128)(2,1)S(1)}, f32[8,128]{1,0:T(8,128)S(1)}) custom-call(bf16[1024,896]{1,0:T(8,128)(2,1)S(1)} %shard_map.49.turned_ref, bf16[224,256]{1,0:T(8,128)(2,1)S(1)} %add_convert_fusion.refs_0_, bf16[224,256]{1,0:T(8,128)(2,1)S(1)} %collective-permute-done.109.refs_1_, ...), custom_call_target="tpu_custom_call" | custom-call | flops 469762048 | bytes 2097152 | tf_op jit(solution)/shard_map/pallas_call | solution.py:449
  96.1 4.3 %collective-permute-start.117 = (bf16[1024,256]{1,0:T(8,128)(2,1)S(1)}, bf16[1024,256]{1,0:T(8,128)(2,1)S(1)}, u32[]{:S(2)}, u32[]{:S(2)}) collective-permute-start(bf16[1024,256]{1,0:T(8,128)(2,1)S(1)} %get-tuple-element.400), channel_id=1, source_target_pairs={{0,4},{4,0},{8,12},{12,8},{16,20},{20,16},{24,28},{28,24},{1,5},{5... | collective-permute-start | bytes 1572872 | tf_op jit(solution)/shard_map/ppermute | solution.py:22
  100.4 3.0 %collective-permute-done.104.refs_2_ = bf16[224,256]{1,0:T(8,128)(2,1)S(1)} collective-permute-done((bf16[224,256]{1,0:T(8,128)(2,1)S(1)}, bf16[224,256]{1,0:T(8,128)(2,1)S(1)}, u32[]{:S(2)}, u32[]{:S(2)}) %collective-permute-start.104) | collective-permute-done | bytes 114720 | tf_op jit(solution)/shard_map/ppermute | solution.py:28
  103.4 1.3 %shard_map.51 = (f32[1024,256]{1,0:T(8,128)S(1)}, bf16[1024,256]{1,0:T(8,128)(2,1)S(1)}, f32[8,128]{1,0:T(8,128)S(1)}) custom-call(bf16[1024,896]{1,0:T(8,128)(2,1)S(1)} %shard_map.49.turned_ref, bf16[224,256]{1,0:T(8,128)(2,1)S(1)} %add_convert_fusion.1.refs_0_, bf16[224,256]{1,0:T(8,128)(2,1)S(1)} %collective-permute-done.103.refs_1_, ...), custom_call_target="tpu_custom_call" | custom-call | flops 469762048 | bytes 2097152 | tf_op jit(solution)/shard_map/pallas_call | solution.py:449
  105.5 1.5 %collective-permute-start.112 = (f32[8,128]{1,0:T(8,128)S(1)}, f32[8,128]{1,0:T(8,128)S(1)}, u32[]{:S(2)}, u32[]{:S(2)}) collective-permute-start(f32[8,128]{1,0:T(8,128)S(1)} %add.284), channel_id=1, source_target_pairs={{0,1},{1,2},{2,3},{3,0},{4,5},{5,6},{6,7},{7,4},{8,9},{9,10},{10,1... | collective-permute-start | bytes 12296 | tf_op jit(solution)/shard_map/ppermute | solution.py:28
  108.6 1.2 %collective-permute-done.112 = f32[8,128]{1,0:T(8,128)S(1)} collective-permute-done((f32[8,128]{1,0:T(8,128)S(1)}, f32[8,128]{1,0:T(8,128)S(1)}, u32[]{:S(2)}, u32[]{:S(2)}) %collective-permute-start.112) | collective-permute-done | bytes 4128 | tf_op jit(solution)/shard_map/ppermute | solution.py:28
  109.9 1.5 %collective-permute-start.115 = (f32[8,128]{1,0:T(8,128)S(1)}, f32[8,128]{1,0:T(8,128)S(1)}, u32[]{:S(2)}, u32[]{:S(2)}) collective-permute-start(f32[8,128]{1,0:T(8,128)S(1)} %add_add_fusion.32.own_ref), channel_id=1, source_target_pairs={{0,4},{4,0},{8,12},{12,8},{16,20},{20,16},{24,28},{28,24},{1,5},{5... | collective-permute-start | bytes 12296 | tf_op jit(solution)/shard_map/ppermute | solution.py:22
  112.2 1.7 %shard_map.53 = f32[1024,512]{1,0:T(8,128)} custom-call(f32[8,128]{1,0:T(8,128)S(1)} %add_add_fusion.32.own_ref, f32[8,128]{1,0:T(8,128)S(1)} %collective-permute-done.115.other_ref, f32[1024,512]{1,0:T(8,128)S(1)} %get-tuple-element.396.halves_ref, f32[1024,256]{1,0:T(8,128)S(1)} %get-tuple-element.397.refs_0_, f32[1024,256]{1,0:T(8,128)S(1)} %get-tuple-element.398.refs_1_, ...), custom_call_target="tpu_custom_call" | custom-call | tf_op jit(solution)/shard_map/pallas_call | solution.py:473
  (59 shorter events, 8.5 us)
Async XLA Ops:
  0.0 36.3 %collective-permute-start.96 = (f32[1024,512]{1,0:T(8,128)}, f32[1024,512]{1,0:T(8,128)}, u32[]{:S(2)}, u32[]{:S(2)}) collective-permute-start(f32[1024,512]{1,0:T(8,128)} %bitcast.11), channel_id=1, source_target_pairs={{0,4},{4,0},{8,12},{12,8},{16,20},{20,16},{24,28},{28,24},{1,5},{5... | collective-permute-start | bytes 6291464 | tf_op jit(solution)/shard_map/ppermute | solution.py:22
  4.7 31.6 %collective-permute-start.97 = (bf16[256,1024]{1,0:T(8,128)(2,1)}, bf16[256,1024]{1,0:T(8,128)(2,1)S(1)}, u32[]{:S(2)}, u32[]{:S(2)}) collective-permute-start(bf16[256,1024]{1,0:T(8,128)(2,1)} %get-tuple-element.376), channel_id=1, source_target_pairs={{0,2},{1,3},{2,0},{3,1},{4,6},{5,7},{6,4},{7,5},{8,10},{9,11},{10,... | collective-permute-start | bytes 1572872 | tf_op jit(solution)/shard_map/ppermute | solution.py:28
  14.9 1.1 copy-start.4
  14.9 1.1 copy-start.5
  15.0 0.9 copy-start.6
  16.7 15.0 %collective-permute-start.26 = (bf16[16,1024]{1,0:T(8,128)(2,1)S(1)}, bf16[16,1024]{1,0:T(8,128)(2,1)S(1)}, u32[]{:S(2)}, u32[]{:S(2)}) collective-permute-start(bf16[16,1024]{1,0:T(8,128)(2,1)S(1)} %slice.191), channel_id=1, source_target_pairs={{1,0},{5,4},{9,8},{13,12},{17,16},{21,20},{25,24},{29,28}} | collective-permute-start | bytes 98312 | tf_op jit(solution)/shard_map/cond/branch_1_fun/ppermute | solution.py:310
  18.0 13.7 %collective-permute-start.25 = (bf16[16,1024]{1,0:T(8,128)(2,1)S(1)}, bf16[16,1024]{1,0:T(8,128)(2,1)S(1)}, u32[]{:S(2)}, u32[]{:S(2)}) collective-permute-start(bf16[16,1024]{1,0:T(8,128)(2,1)S(1)} %slice.190), channel_id=1, source_target_pairs={{1,2},{5,6},{9,10},{13,14},{17,18},{21,22},{25,26},{29,30}} | collective-permute-start | bytes 98312 | tf_op jit(solution)/shard_map/cond/branch_1_fun/ppermute | solution.py:310
  18.7 13.0 %collective-permute-start.24 = (bf16[16,1024]{1,0:T(8,128)(2,1)S(1)}, bf16[16,1024]{1,0:T(8,128)(2,1)S(1)}, u32[]{:S(2)}, u32[]{:S(2)}) collective-permute-start(bf16[16,1024]{1,0:T(8,128)(2,1)S(1)} %slice.189), channel_id=1, source_target_pairs={{1,3},{5,7},{9,11},{13,15},{17,19},{21,23},{25,27},{29,31}} | collective-permute-start | bytes 98312 | tf_op jit(solution)/shard_map/cond/branch_1_fun/ppermute | solution.py:310
  32.5 3.8 %copy-start.1 = (f32[1,1024,512]{2,1,0:T(8,128)S(1)}, f32[1,1024,512]{2,1,0:T(8,128)}, u32[]{:S(2)}) copy-start(f32[1,1024,512]{2,1,0:T(8,128)} %param.42) | copy-start | bytes 6291460
  32.5 3.8 %copy-start.2 = (bf16[1,448,512]{2,1,0:T(8,128)(2,1)S(1)}, bf16[1,448,512]{2,1,0:T(8,128)(2,1)}, u32[]{:S(2)}) copy-start(bf16[1,448,512]{2,1,0:T(8,128)(2,1)} %param.41) | copy-start | bytes 1376260
  32.5 3.8 %copy-start.3 = (s32[1,28]{1,0:T(1,128)S(1)}, s32[1,28]{1,0:T(1,128)}, u32[]{:S(2)}) copy-start(s32[1,28]{1,0:T(1,128)} %lengths_ref.8) | copy-start | bytes 340
  32.5 13.4 %collective-permute-start.98 = (bf16[256,1024]{1,0:T(8,128)(2,1)}, bf16[256,1024]{1,0:T(8,128)(2,1)S(1)}, u32[]{:S(2)}, u32[]{:S(2)}) collective-permute-start(bf16[256,1024]{1,0:T(8,128)(2,1)} %get-tuple-element.382), channel_id=1, source_target_pairs={{0,1},{1,2},{2,3},{3,0},{4,5},{5,6},{6,7},{7,4},{8,9},{9,10},{10,1... | collective-permute-start | bytes 1572872 | tf_op jit(solution)/shard_map/ppermute | solution.py:28
  33.7 24.2 %collective-permute-start.99 = (bf16[256,1024]{1,0:T(8,128)(2,1)}, bf16[256,1024]{1,0:T(8,128)(2,1)S(1)}, u32[]{:S(2)}, u32[]{:S(2)}) collective-permute-start(bf16[256,1024]{1,0:T(8,128)(2,1)} %get-tuple-element.383), channel_id=1, source_target_pairs={{0,3},{1,0},{2,1},{3,2},{4,7},{5,4},{6,5},{7,6},{8,11},{9,8},{10,9... | collective-permute-start | bytes 1572872 | tf_op jit(solution)/shard_map/ppermute | solution.py:28
  36.3 2.0 %copy-start = (bf16[1,448,4096]{2,1,0:T(8,128)(2,1)S(1)}, bf16[1,448,4096]{2,1,0:T(8,128)(2,1)}, u32[]{:S(2)}) copy-start(bf16[1,448,4096]{2,1,0:T(8,128)(2,1)} %param.40) | copy-start | bytes 11010052
  59.5 6.3 %collective-permute-start.106 = (bf16[224,256]{1,0:T(8,128)(2,1)S(1)}, bf16[224,256]{1,0:T(8,128)(2,1)S(1)}, u32[]{:S(2)}, u32[]{:S(2)}) collective-permute-start(bf16[224,256]{1,0:T(8,128)(2,1)S(1)} %get-tuple-element.392), channel_id=1, source_target_pairs={{0,1},{1,2},{2,3},{3,0},{4,5},{5,6},{6,7},{7,4},{8,9},{9,10},{10,1... | collective-permute-start | bytes 344072 | tf_op jit(solution)/shard_map/ppermute | solution.py:28
  62.0 11.3 %collective-permute-start.107 = (bf16[224,256]{1,0:T(8,128)(2,1)S(1)}, bf16[224,256]{1,0:T(8,128)(2,1)S(1)}, u32[]{:S(2)}, u32[]{:S(2)}) collective-permute-start(bf16[224,256]{1,0:T(8,128)(2,1)S(1)} %get-tuple-element.393), channel_id=1, source_target_pairs={{0,2},{1,3},{2,0},{3,1},{4,6},{5,7},{6,4},{7,5},{8,10},{9,11},{10,... | collective-permute-start | bytes 344072 | tf_op jit(solution)/shard_map/ppermute | solution.py:28
  62.0 11.3 %collective-permute-start.108 = (bf16[224,256]{1,0:T(8,128)(2,1)S(1)}, bf16[224,256]{1,0:T(8,128)(2,1)S(1)}, u32[]{:S(2)}, u32[]{:S(2)}) collective-permute-start(bf16[224,256]{1,0:T(8,128)(2,1)S(1)} %get-tuple-element.394), channel_id=1, source_target_pairs={{0,3},{1,0},{2,1},{3,2},{4,7},{5,4},{6,5},{7,6},{8,11},{9,8},{10,9... | collective-permute-start | bytes 344072 | tf_op jit(solution)/shard_map/ppermute | solution.py:28
  64.1 16.2 %collective-permute-start.100 = (bf16[224,256]{1,0:T(8,128)(2,1)S(1)}, bf16[224,256]{1,0:T(8,128)(2,1)S(1)}, u32[]{:S(2)}, u32[]{:S(2)}) collective-permute-start(bf16[224,256]{1,0:T(8,128)(2,1)S(1)} %get-tuple-element.387), channel_id=1, source_target_pairs={{0,1},{1,2},{2,3},{3,0},{4,5},{5,6},{6,7},{7,4},{8,9},{9,10},{10,1... | collective-permute-start | bytes 344072 | tf_op jit(solution)/shard_map/ppermute | solution.py:28
  64.1 17.1 %collective-permute-start.101 = (bf16[224,256]{1,0:T(8,128)(2,1)S(1)}, bf16[224,256]{1,0:T(8,128)(2,1)S(1)}, u32[]{:S(2)}, u32[]{:S(2)}) collective-permute-start(bf16[224,256]{1,0:T(8,128)(2,1)S(1)} %get-tuple-element.388), channel_id=1, source_target_pairs={{0,2},{1,3},{2,0},{3,1},{4,6},{5,7},{6,4},{7,5},{8,10},{9,11},{10,... | collective-permute-start | bytes 344072 | tf_op jit(solution)/shard_map/ppermute | solution.py:28
  65.8 15.4 %collective-permute-start.102 = (bf16[224,256]{1,0:T(8,128)(2,1)S(1)}, bf16[224,256]{1,0:T(8,128)(2,1)S(1)}, u32[]{:S(2)}, u32[]{:S(2)}) collective-permute-start(bf16[224,256]{1,0:T(8,128)(2,1)S(1)} %get-tuple-element.389), channel_id=1, source_target_pairs={{0,3},{1,0},{2,1},{3,2},{4,7},{5,4},{6,5},{7,6},{8,11},{9,8},{10,9... | collective-permute-start | bytes 344072 | tf_op jit(solution)/shard_map/ppermute | solution.py:28
  73.3 16.9 %collective-permute-start.111 = (bf16[224,256]{1,0:T(8,128)(2,1)S(1)}, bf16[224,256]{1,0:T(8,128)(2,1)S(1)}, u32[]{:S(2)}, u32[]{:S(2)}) collective-permute-start(bf16[224,256]{1,0:T(8,128)(2,1)S(1)} %add_convert_fusion.refs_0_), channel_id=1, source_target_pairs={{0,3},{1,0},{2,1},{3,2},{4,7},{5,4},{6,5},{7,6},{8,11},{9,8},{10,9... | collective-permute-start | bytes 344072 | tf_op jit(solution)/shard_map/ppermute | solution.py:28
  73.4 21.5 %collective-permute-start.110 = (bf16[224,256]{1,0:T(8,128)(2,1)S(1)}, bf16[224,256]{1,0:T(8,128)(2,1)S(1)}, u32[]{:S(2)}, u32[]{:S(2)}) collective-permute-start(bf16[224,256]{1,0:T(8,128)(2,1)S(1)} %add_convert_fusion.refs_0_), channel_id=1, source_target_pairs={{0,2},{1,3},{2,0},{3,1},{4,6},{5,7},{6,4},{7,5},{8,10},{9,11},{10,... | collective-permute-start | bytes 344072 | tf_op jit(solution)/shard_map/ppermute | solution.py:28
  80.4 14.5 %collective-permute-start.109 = (bf16[224,256]{1,0:T(8,128)(2,1)S(1)}, bf16[224,256]{1,0:T(8,128)(2,1)S(1)}, u32[]{:S(2)}, u32[]{:S(2)}) collective-permute-start(bf16[224,256]{1,0:T(8,128)(2,1)S(1)} %add_convert_fusion.refs_0_), channel_id=1, source_target_pairs={{0,1},{1,2},{2,3},{3,0},{4,5},{5,6},{6,7},{7,4},{8,9},{9,10},{10,1... | collective-permute-start | bytes 344072 | tf_op jit(solution)/shard_map/ppermute | solution.py:28
  81.3 19.1 %collective-permute-start.105 = (bf16[224,256]{1,0:T(8,128)(2,1)S(1)}, bf16[224,256]{1,0:T(8,128)(2,1)S(1)}, u32[]{:S(2)}, u32[]{:S(2)}) collective-permute-start(bf16[224,256]{1,0:T(8,128)(2,1)S(1)} %add_convert_fusion.1.refs_0_), channel_id=1, source_target_pairs={{0,3},{1,0},{2,1},{3,2},{4,7},{5,4},{6,5},{7,6},{8,11},{9,8},{10,9... | collective-permute-start | bytes 344072 | tf_op jit(solution)/shard_map/ppermute | solution.py:28
  88.2 15.2 %collective-permute-start.104 = (bf16[224,256]{1,0:T(8,128)(2,1)S(1)}, bf16[224,256]{1,0:T(8,128)(2,1)S(1)}, u32[]{:S(2)}, u32[]{:S(2)}) collective-permute-start(bf16[224,256]{1,0:T(8,128)(2,1)S(1)} %add_convert_fusion.1.refs_0_), channel_id=1, source_target_pairs={{0,2},{1,3},{2,0},{3,1},{4,6},{5,7},{6,4},{7,5},{8,10},{9,11},{10,... | collective-permute-start | bytes 344072 | tf_op jit(solution)/shard_map/ppermute | solution.py:28
  90.2 13.2 %collective-permute-start.103 = (bf16[224,256]{1,0:T(8,128)(2,1)S(1)}, bf16[224,256]{1,0:T(8,128)(2,1)S(1)}, u32[]{:S(2)}, u32[]{:S(2)}) collective-permute-start(bf16[224,256]{1,0:T(8,128)(2,1)S(1)} %add_convert_fusion.1.refs_0_), channel_id=1, source_target_pairs={{0,1},{1,2},{2,3},{3,0},{4,5},{5,6},{6,7},{7,4},{8,9},{9,10},{10,1... | collective-permute-start | bytes 344072 | tf_op jit(solution)/shard_map/ppermute | solution.py:28
  96.1 16.1 %collective-permute-start.117 = (bf16[1024,256]{1,0:T(8,128)(2,1)S(1)}, bf16[1024,256]{1,0:T(8,128)(2,1)S(1)}, u32[]{:S(2)}, u32[]{:S(2)}) collective-permute-start(bf16[1024,256]{1,0:T(8,128)(2,1)S(1)} %get-tuple-element.400), channel_id=1, source_target_pairs={{0,4},{4,0},{8,12},{12,8},{16,20},{20,16},{24,28},{28,24},{1,5},{5... | collective-permute-start | bytes 1572872 | tf_op jit(solution)/shard_map/ppermute | solution.py:22
  104.7 7.5 %collective-permute-start.116 = (bf16[1024,256]{1,0:T(8,128)(2,1)S(1)}, bf16[1024,256]{1,0:T(8,128)(2,1)S(1)}, u32[]{:S(2)}, u32[]{:S(2)}) collective-permute-start(bf16[1024,256]{1,0:T(8,128)(2,1)S(1)} %get-tuple-element.399), channel_id=1, source_target_pairs={{0,4},{4,0},{8,12},{12,8},{16,20},{20,16},{24,28},{28,24},{1,5},{5... | collective-permute-start | bytes 1572872 | tf_op jit(solution)/shard_map/ppermute | solution.py:22
  105.3 2.5 %collective-permute-start.114 = (f32[8,128]{1,0:T(8,128)S(1)}, f32[8,128]{1,0:T(8,128)S(1)}, u32[]{:S(2)}, u32[]{:S(2)}) collective-permute-start(f32[8,128]{1,0:T(8,128)S(1)} %add.284), channel_id=1, source_target_pairs={{0,3},{1,0},{2,1},{3,2},{4,7},{5,4},{6,5},{7,6},{8,11},{9,8},{10,9... | collective-permute-start | bytes 12296 | tf_op jit(solution)/shard_map/ppermute | solution.py:28
  105.3 3.4 %collective-permute-start.113 = (f32[8,128]{1,0:T(8,128)S(1)}, f32[8,128]{1,0:T(8,128)S(1)}, u32[]{:S(2)}, u32[]{:S(2)}) collective-permute-start(f32[8,128]{1,0:T(8,128)S(1)} %add.284), channel_id=1, source_target_pairs={{0,2},{1,3},{2,0},{3,1},{4,6},{5,7},{6,4},{7,5},{8,10},{9,11},{10,... | collective-permute-start | bytes 12296 | tf_op jit(solution)/shard_map/ppermute | solution.py:28
  105.5 4.4 %collective-permute-start.112 = (f32[8,128]{1,0:T(8,128)S(1)}, f32[8,128]{1,0:T(8,128)S(1)}, u32[]{:S(2)}, u32[]{:S(2)}) collective-permute-start(f32[8,128]{1,0:T(8,128)S(1)} %add.284), channel_id=1, source_target_pairs={{0,1},{1,2},{2,3},{3,0},{4,5},{5,6},{6,7},{7,4},{8,9},{9,10},{10,1... | collective-permute-start | bytes 12296 | tf_op jit(solution)/shard_map/ppermute | solution.py:28
  109.9 2.3 %collective-permute-start.115 = (f32[8,128]{1,0:T(8,128)S(1)}, f32[8,128]{1,0:T(8,128)S(1)}, u32[]{:S(2)}, u32[]{:S(2)}) collective-permute-start(f32[8,128]{1,0:T(8,128)S(1)} %add_add_fusion.32.own_ref), channel_id=1, source_target_pairs={{0,4},{4,0},{8,12},{12,8},{16,20},{20,16},{24,28},{28,24},{1,5},{5... | collective-permute-start | bytes 12296 | tf_op jit(solution)/shard_map/ppermute | solution.py:22
  (2 other events, 1.5 us)
where the time goes:
time: 115 us; the launch traced here: 114 us
  starting transfers between devices  42.5 us (37%)
  waiting for transfers between devices  40.2 us (35%)
  Pallas kernels  23.6 us (21%)
  local copies, waits for them, and re-layouts  4.57 us (4%)
  between operations  2.9 us (3%)
    ppermute x18, starting transfers between devices, turned(): return lax.ppermute(value, 'fsdp', ring)  32.8 us
    ppermute x18, waiting for transfers between devices, turned(): return lax.ppermute(value, 'fsdp', ring)  27.1 us
    ppermute x3, waiting for transfers between devices, more_rows(): lax.ppermute(block[:size], 'fsdp', [(source, (source + i) % members)])  12.3 us
    pallas_call x2, Pallas kernels, sent_to(): pl.pallas_call(functools.partial(sent_kernel, members, offsets, sizes), i...  9.26 us
    pallas_call x1, Pallas kernels, local(): pl.pallas_call(functools.partial(own_kernel, members, far, scale), in_spe...  7.21 us
    ppermute x4, starting transfers between devices, swapped(): return lax.ppermute(value, axis, pairs)  7.04 us
    unnamed x18, local copies, waits for them, and re-layouts  4.47 us
    ppermute x3, starting transfers between devices, more_rows(): lax.ppermute(block[:size], 'fsdp', [(source, (source + i) % members)])  2.61 us
  transfers between devices with their start and end apart: 25, of which 11 were waited for; matrix products, arithmetic and copies ran while one was open for 0% of the time, Pallas kernels for 18%

commit v1 on v0

--- a/solution.py
+++ b/solution.py
@@ -334,7 +334,7 @@
     anywhere = pl.BlockSpec(memory_space=pl.ANY)
     smem = pl.BlockSpec(memory_space=pltpu.SMEM)
     params = pltpu.CompilerParams(vmem_limit_bytes=16 * 2**20)
-    middle = pltpu.CompilerParams(vmem_limit_bytes=24 * 2**20)
+    middle = pltpu.CompilerParams(vmem_limit_bytes=40 * 2**20)
     large = pltpu.CompilerParams(vmem_limit_bytes=56 * 2**20)
 
     def array(rows, width, dtype):

time: 115 us -> 118 us (1.026)
  starting transfers between devices: 42.5 us -> 47.4 us
  waiting for transfers between devices: 40.2 us -> 36.7 us
    ppermute x3 -> x6, starting transfers between devices: 2.61 us -> 11.6 us  [more_rows(): lax.ppermute(block[:size], 'fsdp', [(source, (source + i) % members)])]
    ppermute x18, waiting for transfers between devices: 27.1 us -> 20.3 us  [turned(): return lax.ppermute(value, 'fsdp', ring)]
    ppermute x4, starting transfers between devices: 7.04 us -> 2.8 us  [swapped(): return lax.ppermute(value, axis, pairs)]
    ppermute x3 -> x6, waiting for transfers between devices: 12.3 us -> 15.5 us  [more_rows(): lax.ppermute(block[:size], 'fsdp', [(source, (source + i) % members)])]
    unnamed x18 -> x16, local copies, waits for them, and re-layouts: 4.47 us -> 2.43 us
    slice x3 -> x6, local copies, waits for them, and re-layouts: 0.01 us -> 1.98 us  [more_rows(): block[:size]]
  transfers between devices with their start and end apart: 25 -> 28, of which waited for: 11 -> 10; matrix products, arithmetic and copies ran while one was open for 0% -> 2% of each run, Pallas kernels for 18% -> 18%
where the time goes in v1:
time: 118 us; the launch traced here: 117 us
  starting transfers between devices  47.4 us (40%)
  waiting for transfers between devices  36.7 us (31%)
  Pallas kernels  24.6 us (21%)
  local copies, waits for them, and re-layouts  4.54 us (4%)
  between operations  3.18 us (3%)
    ppermute x18, starting transfers between devices, turned(): return lax.ppermute(value, 'fsdp', ring)  33 us
    ppermute x18, waiting for transfers between devices, turned(): return lax.ppermute(value, 'fsdp', ring)  20.3 us
    ppermute x6, waiting for transfers between devices, more_rows(): lax.ppermute(block[:size], 'fsdp', [(source, (source + i) % members)])  15.5 us
    ppermute x6, starting transfers between devices, more_rows(): lax.ppermute(block[:size], 'fsdp', [(source, (source + i) % members)])  11.6 us
    pallas_call x2, Pallas kernels, sent_to(): pl.pallas_call(functools.partial(sent_kernel, members, offsets, sizes), i...  9.99 us
    pallas_call x1, Pallas kernels, local(): pl.pallas_call(functools.partial(own_kernel, members, far, scale), in_spe...  7.41 us
    ppermute x4, starting transfers between devices, swapped(): return lax.ppermute(value, axis, pairs)  2.8 us
    pallas_call x2, Pallas kernels, local(): pl.pallas_call(functools.partial(gradient_kernel, members), in_specs=[vme...  2.55 us
  transfers between devices with their start and end apart: 28, of which 10 were waited for; matrix products, arithmetic and copies ran while one was open for 2% of the time, Pallas kernels for 18%

profile of v1, /device:TPU:7, one launch (start us, length us, event | category | flops | bytes accessed | tf_op | source)
XLA Modules:
  0.0 116.9 jit_solution(10343206807316528404)
XLA Ops:
  0.7 4.0 %shard_map.47 = (bf16[256,1024]{1,0:T(8,128)(2,1)}, bf16[208,1024]{1,0:T(8,128)(2,1)S(1)}, s32[1]{0:T(128)}) custom-call(s32[1,28]{1,0:T(1,128)} %lengths_ref.8, bf16[448,4096]{1,0:T(8,128)(2,1)} %bitcast.11), custom_call_target="tpu_custom_call" | custom-call | flops 234881024 | bytes 1441792 | tf_op jit(solution)/shard_map/pallas_call | solution.py:349
  4.7 2.4 %collective-permute-start.97 = (bf16[256,1024]{1,0:T(8,128)(2,1)}, bf16[256,1024]{1,0:T(8,128)(2,1)S(1)}, u32[]{:S(2)}, u32[]{:S(2)}) collective-permute-start(bf16[256,1024]{1,0:T(8,128)(2,1)} %get-tuple-element.376), channel_id=1, source_target_pairs={{0,2},{1,3},{2,0},{3,1},{4,6},{5,7},{6,4},{7,5},{8,10},{9,11},{10,... | collective-permute-start | bytes 1572872 | tf_op jit(solution)/shard_map/ppermute | solution.py:28
  9.8 6.0 %shard_map.46 = (bf16[256,1024]{1,0:T(8,128)(2,1)}, bf16[256,1024]{1,0:T(8,128)(2,1)}, bf16[208,1024]{1,0:T(8,128)(2,1)S(1)}, bf16[208,1024]{1,0:T(8,128)(2,1)S(1)}, s32[1]{0:T(128)}) custom-call(s32[1,28]{1,0:T(1,128)} %lengths_ref.8, bf16[448,4096]{1,0:T(8,128)(2,1)} %bitcast.12), custom_call_target="tpu_custom_call" | custom-call | flops 469762048 | bytes 2883584 | tf_op jit(solution)/shard_map/pallas_call | solution.py:349
  17.7 14.9 %conditional.5 = (bf16[208,1024]{1,0:T(8,128)(2,1)S(1)}) conditional(s32[]{:T(128)} %bitcast.2, bf16[208,1024]{1,0:T(8,128)(2,1)S(1)} %get-tuple-element.372, (bf16[208,1024]{1,0:T(8,128)(2,1)S(1)}, bf16[208,1024]{1,0:T(8,128)(2,1)S(1)}, bf16[208,1024]{1,0:T(8,128)(2,1)S(1)}) %tuple.114, ...), branch_computations={%region_9.10_spmd, %region_10.11_spmd, %region_11.12_spmd, %region... | conditional | flops 425984 | bytes 6815872 | solution.py:381
  17.7 1.3 %collective-permute-start.29 = (bf16[32,1024]{1,0:T(8,128)(2,1)S(1)}, bf16[32,1024]{1,0:T(8,128)(2,1)S(1)}, u32[]{:S(2)}, u32[]{:S(2)}) collective-permute-start(bf16[32,1024]{1,0:T(8,128)(2,1)S(1)} %slice.194), channel_id=1, source_target_pairs={{1,0},{5,4},{9,8},{13,12},{17,16},{21,20},{25,24},{29,28}} | collective-permute-start | bytes 196616 | tf_op jit(solution)/shard_map/cond/branch_2_fun/ppermute | solution.py:310
  20.4 12.1 %collective-permute-done.29 = bf16[32,1024]{1,0:T(8,128)(2,1)S(1)} collective-permute-done((bf16[32,1024]{1,0:T(8,128)(2,1)S(1)}, bf16[32,1024]{1,0:T(8,128)(2,1)S(1)}, u32[]{:S(2)}, u32[]{:S(2)}) %collective-permute-start.29) | collective-permute-done | bytes 65568 | tf_op jit(solution)/shard_map/cond/branch_2_fun/ppermute | solution.py:310
  33.3 14.7 %conditional.4 = (bf16[208,1024]{1,0:T(8,128)(2,1)S(1)}) conditional(s32[]{:T(128)} %bitcast.1, bf16[208,1024]{1,0:T(8,128)(2,1)S(1)} %get-tuple-element.372, (bf16[208,1024]{1,0:T(8,128)(2,1)S(1)}, bf16[208,1024]{1,0:T(8,128)(2,1)}, bf16[208,1024]{1,0:T(8,128)(2,1)}) %tuple.160, (bf16[208,1024]{1,0:T(8,128)(2,1)S(1)}, ...), branch_computations={%region_0.0_spmd, %region_1.2_spmd, %region_2.3_spmd, %region_3.4_... | conditional | flops 425984 | bytes 6815872 | solution.py:381
  34.4 6.5 %collective-permute-start.8 = (bf16[48,1024]{1,0:T(8,128)(2,1)S(1)}, bf16[48,1024]{1,0:T(8,128)(2,1)S(1)}, u32[]{:S(2)}, u32[]{:S(2)}) collective-permute-start(bf16[48,1024]{1,0:T(8,128)(2,1)S(1)} %slice.176), channel_id=1, source_target_pairs={{0,3},{4,7},{8,11},{12,15},{16,19},{20,23},{24,27},{28,31}} | collective-permute-start | bytes 294920 | tf_op jit(solution)/shard_map/cond/branch_3_fun/ppermute | solution.py:310
  41.7 1.3 %collective-permute-start.7 = (bf16[48,1024]{1,0:T(8,128)(2,1)S(1)}, bf16[48,1024]{1,0:T(8,128)(2,1)S(1)}, u32[]{:S(2)}, u32[]{:S(2)}) collective-permute-start(bf16[48,1024]{1,0:T(8,128)(2,1)S(1)} %slice.175), channel_id=1, source_target_pairs={{0,1},{4,5},{8,9},{12,13},{16,17},{20,21},{24,25},{28,29}} | collective-permute-start | bytes 294920 | tf_op jit(solution)/shard_map/cond/branch_3_fun/ppermute | solution.py:310
  43.0 1.3 %collective-permute-start.6 = (bf16[48,1024]{1,0:T(8,128)(2,1)S(1)}, bf16[48,1024]{1,0:T(8,128)(2,1)S(1)}, u32[]{:S(2)}, u32[]{:S(2)}) collective-permute-start(bf16[48,1024]{1,0:T(8,128)(2,1)S(1)} %slice.174), channel_id=1, source_target_pairs={{0,2},{4,6},{8,10},{12,14},{16,18},{20,22},{24,26},{28,30}} | collective-permute-start | bytes 294920 | tf_op jit(solution)/shard_map/cond/branch_3_fun/ppermute | solution.py:310
  44.3 1.3 %collective-permute-done.7 = bf16[48,1024]{1,0:T(8,128)(2,1)S(1)} collective-permute-done((bf16[48,1024]{1,0:T(8,128)(2,1)S(1)}, bf16[48,1024]{1,0:T(8,128)(2,1)S(1)}, u32[]{:S(2)}, u32[]{:S(2)}) %collective-permute-start.7) | collective-permute-done | bytes 98336 | tf_op jit(solution)/shard_map/cond/branch_3_fun/ppermute | solution.py:310
  45.7 2.1 %collective-permute-done.6 = bf16[48,1024]{1,0:T(8,128)(2,1)S(1)} collective-permute-done((bf16[48,1024]{1,0:T(8,128)(2,1)S(1)}, bf16[48,1024]{1,0:T(8,128)(2,1)S(1)}, u32[]{:S(2)}, u32[]{:S(2)}) %collective-permute-start.6) | collective-permute-done | bytes 98336 | tf_op jit(solution)/shard_map/cond/branch_3_fun/ppermute | solution.py:310
  48.2 3.2 %collective-permute-start.99 = (bf16[256,1024]{1,0:T(8,128)(2,1)}, bf16[256,1024]{1,0:T(8,128)(2,1)S(1)}, u32[]{:S(2)}, u32[]{:S(2)}) collective-permute-start(bf16[256,1024]{1,0:T(8,128)(2,1)} %get-tuple-element.383), channel_id=1, source_target_pairs={{0,3},{1,0},{2,1},{3,2},{4,7},{5,4},{6,5},{7,6},{8,11},{9,8},{10,9... | collective-permute-start | bytes 1572872 | tf_op jit(solution)/shard_map/ppermute | solution.py:28
  51.4 7.4 %shard_map.48 = (bf16[1360,1024]{1,0:T(8,128)(2,1)S(1)}, f32[1360,512]{1,0:T(8,128)S(1)}, bf16[1024,512]{1,0:T(8,128)(2,1)S(1)}, f32[1024,512]{1,0:T(8,128)S(1)}) custom-call(s32[1,28]{1,0:T(1,128)S(1)} %copy-done.2, bf16[448,4096]{1,0:T(8,128)(2,1)} %bitcast.13, bf16[448,512]{1,0:T(8,128)(2,1)S(1)} %bitcast.10, f32[1024,512]{1,0:T(8,128)S(1)} %bitcast.9, ...), custom_call_target="tpu_custom_call" | custom-call | flops 2047868928 | bytes 10485760 | tf_op jit(solution)/shard_map/pallas_call | solution.py:392
  58.8 10.6 %collective-permute-done.99.refs_1_ = bf16[256,1024]{1,0:T(8,128)(2,1)S(1)} collective-permute-done((bf16[256,1024]{1,0:T(8,128)(2,1)}, bf16[256,1024]{1,0:T(8,128)(2,1)S(1)}, u32[]{:S(2)}, u32[]{:S(2)}) %collective-permute-start.99) | collective-permute-done | bytes 524320 | tf_op jit(solution)/shard_map/ppermute | solution.py:28
  69.4 1.6 %shard_map.50 = (f32[224,256]{1,0:T(8,128)S(1)}, bf16[224,256]{1,0:T(8,128)(2,1)S(1)}, bf16[224,256]{1,0:T(8,128)(2,1)S(1)}, bf16[224,256]{1,0:T(8,128)(2,1)S(1)...) custom-call(s32[1,28]{1,0:T(1,128)S(1)} %copy-done.2, ...), custom_call_target="tpu_custom_call", output_to_operand_aliasing={{8}: (2, {})} | custom-call | flops 536870912 | bytes 5570560 | tf_op jit(solution)/shard_map/pallas_call | solution.py:419
  71.0 2.6 %collective-permute-start.106 = (bf16[224,256]{1,0:T(8,128)(2,1)S(1)}, bf16[224,256]{1,0:T(8,128)(2,1)S(1)}, u32[]{:S(2)}, u32[]{:S(2)}) collective-permute-start(bf16[224,256]{1,0:T(8,128)(2,1)S(1)} %get-tuple-element.392), channel_id=1, source_target_pairs={{0,1},{1,2},{2,3},{3,0},{4,5},{5,6},{6,7},{7,4},{8,9},{9,10},{10,1... | collective-permute-start | bytes 344072 | tf_op jit(solution)/shard_map/ppermute | solution.py:28
  74.6 2.3 %collective-permute-start.108 = (bf16[224,256]{1,0:T(8,128)(2,1)S(1)}, bf16[224,256]{1,0:T(8,128)(2,1)S(1)}, u32[]{:S(2)}, u32[]{:S(2)}) collective-permute-start(bf16[224,256]{1,0:T(8,128)(2,1)S(1)} %get-tuple-element.394), channel_id=1, source_target_pairs={{0,3},{1,0},{2,1},{3,2},{4,7},{5,4},{6,5},{7,6},{8,11},{9,8},{10,9... | collective-permute-start | bytes 344072 | tf_op jit(solution)/shard_map/ppermute | solution.py:28
  77.4 2.8 %collective-permute-start.102 = (bf16[224,256]{1,0:T(8,128)(2,1)S(1)}, bf16[224,256]{1,0:T(8,128)(2,1)S(1)}, u32[]{:S(2)}, u32[]{:S(2)}) collective-permute-start(bf16[224,256]{1,0:T(8,128)(2,1)S(1)} %get-tuple-element.389), channel_id=1, source_target_pairs={{0,3},{1,0},{2,1},{3,2},{4,7},{5,4},{6,5},{7,6},{8,11},{9,8},{10,9... | collective-permute-start | bytes 344072 | tf_op jit(solution)/shard_map/ppermute | solution.py:28
  80.2 3.2 %collective-permute-done.107 = bf16[224,256]{1,0:T(8,128)(2,1)S(1)} collective-permute-done((bf16[224,256]{1,0:T(8,128)(2,1)S(1)}, bf16[224,256]{1,0:T(8,128)(2,1)S(1)}, u32[]{:S(2)}, u32[]{:S(2)}) %collective-permute-start.107) | collective-permute-done | bytes 114720 | tf_op jit(solution)/shard_map/ppermute | solution.py:28
  83.5 8.2 %collective-permute-start.111 = (bf16[224,256]{1,0:T(8,128)(2,1)S(1)}, bf16[224,256]{1,0:T(8,128)(2,1)S(1)}, u32[]{:S(2)}, u32[]{:S(2)}) collective-permute-start(bf16[224,256]{1,0:T(8,128)(2,1)S(1)} %add_convert_fusion.refs_0_), channel_id=1, source_target_pairs={{0,3},{1,0},{2,1},{3,2},{4,7},{5,4},{6,5},{7,6},{8,11},{9,8},{10,9... | collective-permute-start | bytes 344072 | tf_op jit(solution)/shard_map/ppermute | solution.py:28
  93.2 5.9 %collective-permute-start.105 = (bf16[224,256]{1,0:T(8,128)(2,1)S(1)}, bf16[224,256]{1,0:T(8,128)(2,1)S(1)}, u32[]{:S(2)}, u32[]{:S(2)}) collective-permute-start(bf16[224,256]{1,0:T(8,128)(2,1)S(1)} %add_convert_fusion.1.refs_0_), channel_id=1, source_target_pairs={{0,3},{1,0},{2,1},{3,2},{4,7},{5,4},{6,5},{7,6},{8,11},{9,8},{10,9... | collective-permute-start | bytes 344072 | tf_op jit(solution)/shard_map/ppermute | solution.py:28
  99.5 1.3 %shard_map.49.turned_ref = bf16[1024,896]{1,0:T(8,128)(2,1)S(1)} custom-call(s32[1,28]{1,0:T(1,128)S(1)} %copy-done.2, bf16[1360,1024]{1,0:T(8,128)(2,1)S(1)} %get-tuple-element.381.rows_ref, bf16[256,1024]{1,0:T(8,128)(2,1)S(1)} %collective-permute-done.98.refs_0_, bf16[256,1024]{1,0:T(8,128)(2,1)S(1)} %collective-permute-done.99.refs_1_), custom_call_target="tpu_custom_call" | custom-call | bytes 3670016 | tf_op jit(solution)/shard_map/pallas_call | solution.py:432
  100.8 1.3 %shard_map.52 = (f32[1024,256]{1,0:T(8,128)S(1)}, bf16[1024,256]{1,0:T(8,128)(2,1)S(1)}, f32[8,128]{1,0:T(8,128)S(1)}) custom-call(bf16[1024,896]{1,0:T(8,128)(2,1)S(1)} %shard_map.49.turned_ref, bf16[224,256]{1,0:T(8,128)(2,1)S(1)} %add_convert_fusion.refs_0_, bf16[224,256]{1,0:T(8,128)(2,1)S(1)} %collective-permute-done.109.refs_1_, ...), custom_call_target="tpu_custom_call" | custom-call | flops 469762048 | bytes 2097152 | tf_op jit(solution)/shard_map/pallas_call | solution.py:449
  102.2 2.8 %collective-permute-done.104.refs_2_ = bf16[224,256]{1,0:T(8,128)(2,1)S(1)} collective-permute-done((bf16[224,256]{1,0:T(8,128)(2,1)S(1)}, bf16[224,256]{1,0:T(8,128)(2,1)S(1)}, u32[]{:S(2)}, u32[]{:S(2)}) %collective-permute-start.104) | collective-permute-done | bytes 114720 | tf_op jit(solution)/shard_map/ppermute | solution.py:28
  105.0 1.3 %shard_map.51 = (f32[1024,256]{1,0:T(8,128)S(1)}, bf16[1024,256]{1,0:T(8,128)(2,1)S(1)}, f32[8,128]{1,0:T(8,128)S(1)}) custom-call(bf16[1024,896]{1,0:T(8,128)(2,1)S(1)} %shard_map.49.turned_ref, bf16[224,256]{1,0:T(8,128)(2,1)S(1)} %add_convert_fusion.1.refs_0_, bf16[224,256]{1,0:T(8,128)(2,1)S(1)} %collective-permute-done.103.refs_1_, ...), custom_call_target="tpu_custom_call" | custom-call | flops 469762048 | bytes 2097152 | tf_op jit(solution)/shard_map/pallas_call | solution.py:449
  106.3 1.3 %collective-permute-start.114 = (f32[8,128]{1,0:T(8,128)S(1)}, f32[8,128]{1,0:T(8,128)S(1)}, u32[]{:S(2)}, u32[]{:S(2)}) collective-permute-start(f32[8,128]{1,0:T(8,128)S(1)} %add.284), channel_id=1, source_target_pairs={{0,3},{1,0},{2,1},{3,2},{4,7},{5,4},{6,5},{7,6},{8,11},{9,8},{10,9... | collective-permute-start | bytes 12296 | tf_op jit(solution)/shard_map/ppermute | solution.py:28
  108.0 1.4 %collective-permute-start.112 = (f32[8,128]{1,0:T(8,128)S(1)}, f32[8,128]{1,0:T(8,128)S(1)}, u32[]{:S(2)}, u32[]{:S(2)}) collective-permute-start(f32[8,128]{1,0:T(8,128)S(1)} %add.284), channel_id=1, source_target_pairs={{0,1},{1,2},{2,3},{3,0},{4,5},{5,6},{6,7},{7,4},{8,9},{9,10},{10,1... | collective-permute-start | bytes 12296 | tf_op jit(solution)/shard_map/ppermute | solution.py:28
  109.4 1.6 %collective-permute-done.113 = f32[8,128]{1,0:T(8,128)S(1)} collective-permute-done((f32[8,128]{1,0:T(8,128)S(1)}, f32[8,128]{1,0:T(8,128)S(1)}, u32[]{:S(2)}, u32[]{:S(2)}) %collective-permute-start.113) | collective-permute-done | bytes 4128 | tf_op jit(solution)/shard_map/ppermute | solution.py:28
  111.0 1.3 %collective-permute-done.112 = f32[8,128]{1,0:T(8,128)S(1)} collective-permute-done((f32[8,128]{1,0:T(8,128)S(1)}, f32[8,128]{1,0:T(8,128)S(1)}, u32[]{:S(2)}, u32[]{:S(2)}) %collective-permute-start.112) | collective-permute-done | bytes 4128 | tf_op jit(solution)/shard_map/ppermute | solution.py:28
  112.3 2.0 %collective-permute-start.115 = (f32[8,128]{1,0:T(8,128)S(1)}, f32[8,128]{1,0:T(8,128)S(1)}, u32[]{:S(2)}, u32[]{:S(2)}) collective-permute-start(f32[8,128]{1,0:T(8,128)S(1)} %add_add_fusion.32.own_ref), channel_id=1, source_target_pairs={{0,4},{4,0},{8,12},{12,8},{16,20},{20,16},{24,28},{28,24},{1,5},{5... | collective-permute-start | bytes 12296 | tf_op jit(solution)/shard_map/ppermute | solution.py:22
  115.1 1.7 %shard_map.53 = f32[1024,512]{1,0:T(8,128)} custom-call(f32[8,128]{1,0:T(8,128)S(1)} %add_add_fusion.32.own_ref, f32[8,128]{1,0:T(8,128)S(1)} %collective-permute-done.115.other_ref, f32[1024,512]{1,0:T(8,128)S(1)} %get-tuple-element.396.halves_ref, f32[1024,256]{1,0:T(8,128)S(1)} %get-tuple-element.397.refs_0_, f32[1024,256]{1,0:T(8,128)S(1)} %get-tuple-element.398.refs_1_, ...), custom_call_target="tpu_custom_call" | custom-call | tf_op jit(solution)/shard_map/pallas_call | solution.py:473
  (68 shorter events, 11.7 us)
Async XLA Ops:
  0.0 51.3 %collective-permute-start.96 = (f32[1024,512]{1,0:T(8,128)}, f32[1024,512]{1,0:T(8,128)}, u32[]{:S(2)}, u32[]{:S(2)}) collective-permute-start(f32[1024,512]{1,0:T(8,128)} %bitcast.8), channel_id=1, source_target_pairs={{0,4},{4,0},{8,12},{12,8},{16,20},{20,16},{24,28},{28,24},{1,5},{5... | collective-permute-start | bytes 6291464 | tf_op jit(solution)/shard_map/ppermute | solution.py:22
  4.7 46.6 %collective-permute-start.97 = (bf16[256,1024]{1,0:T(8,128)(2,1)}, bf16[256,1024]{1,0:T(8,128)(2,1)S(1)}, u32[]{:S(2)}, u32[]{:S(2)}) collective-permute-start(bf16[256,1024]{1,0:T(8,128)(2,1)} %get-tuple-element.376), channel_id=1, source_target_pairs={{0,2},{1,3},{2,0},{3,1},{4,6},{5,7},{6,4},{7,5},{8,10},{9,11},{10,... | collective-permute-start | bytes 1572872 | tf_op jit(solution)/shard_map/ppermute | solution.py:28
  15.8 1.1 copy-start.3
  17.7 14.8 %collective-permute-start.29 = (bf16[32,1024]{1,0:T(8,128)(2,1)S(1)}, bf16[32,1024]{1,0:T(8,128)(2,1)S(1)}, u32[]{:S(2)}, u32[]{:S(2)}) collective-permute-start(bf16[32,1024]{1,0:T(8,128)(2,1)S(1)} %slice.194), channel_id=1, source_target_pairs={{1,0},{5,4},{9,8},{13,12},{17,16},{21,20},{25,24},{29,28}} | collective-permute-start | bytes 196616 | tf_op jit(solution)/shard_map/cond/branch_2_fun/ppermute | solution.py:310
  19.0 13.5 %collective-permute-start.28 = (bf16[32,1024]{1,0:T(8,128)(2,1)S(1)}, bf16[32,1024]{1,0:T(8,128)(2,1)S(1)}, u32[]{:S(2)}, u32[]{:S(2)}) collective-permute-start(bf16[32,1024]{1,0:T(8,128)(2,1)S(1)} %slice.193), channel_id=1, source_target_pairs={{1,2},{5,6},{9,10},{13,14},{17,18},{21,22},{25,26},{29,30}} | collective-permute-start | bytes 196616 | tf_op jit(solution)/shard_map/cond/branch_2_fun/ppermute | solution.py:310
  19.7 12.8 %collective-permute-start.27 = (bf16[32,1024]{1,0:T(8,128)(2,1)S(1)}, bf16[32,1024]{1,0:T(8,128)(2,1)S(1)}, u32[]{:S(2)}, u32[]{:S(2)}) collective-permute-start(bf16[32,1024]{1,0:T(8,128)(2,1)S(1)} %slice.192), channel_id=1, source_target_pairs={{1,3},{5,7},{9,11},{13,15},{17,19},{21,23},{25,27},{29,31}} | collective-permute-start | bytes 196616 | tf_op jit(solution)/shard_map/cond/branch_2_fun/ppermute | solution.py:310
  33.3 18.0 %copy-start = (f32[1,1024,512]{2,1,0:T(8,128)S(1)}, f32[1,1024,512]{2,1,0:T(8,128)}, u32[]{:S(2)}) copy-start(f32[1,1024,512]{2,1,0:T(8,128)} %param.42) | copy-start | bytes 6291460
  33.3 18.1 %copy-start.1 = (bf16[1,448,512]{2,1,0:T(8,128)(2,1)S(1)}, bf16[1,448,512]{2,1,0:T(8,128)(2,1)}, u32[]{:S(2)}) copy-start(bf16[1,448,512]{2,1,0:T(8,128)(2,1)} %param.41) | copy-start | bytes 1376260
  33.3 18.1 %copy-start.2 = (s32[1,28]{1,0:T(1,128)S(1)}, s32[1,28]{1,0:T(1,128)}, u32[]{:S(2)}) copy-start(s32[1,28]{1,0:T(1,128)} %lengths_ref.8) | copy-start | bytes 340
  34.4 10.0 %collective-permute-start.8 = (bf16[48,1024]{1,0:T(8,128)(2,1)S(1)}, bf16[48,1024]{1,0:T(8,128)(2,1)S(1)}, u32[]{:S(2)}, u32[]{:S(2)}) collective-permute-start(bf16[48,1024]{1,0:T(8,128)(2,1)S(1)} %slice.176), channel_id=1, source_target_pairs={{0,3},{4,7},{8,11},{12,15},{16,19},{20,23},{24,27},{28,31}} | collective-permute-start | bytes 294920 | tf_op jit(solution)/shard_map/cond/branch_3_fun/ppermute | solution.py:310
  41.7 3.9 %collective-permute-start.7 = (bf16[48,1024]{1,0:T(8,128)(2,1)S(1)}, bf16[48,1024]{1,0:T(8,128)(2,1)S(1)}, u32[]{:S(2)}, u32[]{:S(2)}) collective-permute-start(bf16[48,1024]{1,0:T(8,128)(2,1)S(1)} %slice.175), channel_id=1, source_target_pairs={{0,1},{4,5},{8,9},{12,13},{16,17},{20,21},{24,25},{28,29}} | collective-permute-start | bytes 294920 | tf_op jit(solution)/shard_map/cond/branch_3_fun/ppermute | solution.py:310
  43.0 4.7 %collective-permute-start.6 = (bf16[48,1024]{1,0:T(8,128)(2,1)S(1)}, bf16[48,1024]{1,0:T(8,128)(2,1)S(1)}, u32[]{:S(2)}, u32[]{:S(2)}) collective-permute-start(bf16[48,1024]{1,0:T(8,128)(2,1)S(1)} %slice.174), channel_id=1, source_target_pairs={{0,2},{4,6},{8,10},{12,14},{16,18},{20,22},{24,26},{28,30}} | collective-permute-start | bytes 294920 | tf_op jit(solution)/shard_map/cond/branch_3_fun/ppermute | solution.py:310
  48.0 10.8 %collective-permute-start.98 = (bf16[256,1024]{1,0:T(8,128)(2,1)}, bf16[256,1024]{1,0:T(8,128)(2,1)S(1)}, u32[]{:S(2)}, u32[]{:S(2)}) collective-permute-start(bf16[256,1024]{1,0:T(8,128)(2,1)} %get-tuple-element.382), channel_id=1, source_target_pairs={{0,1},{1,2},{2,3},{3,0},{4,5},{5,6},{6,7},{7,4},{8,9},{9,10},{10,1... | collective-permute-start | bytes 1572872 | tf_op jit(solution)/shard_map/ppermute | solution.py:28
  48.2 21.2 %collective-permute-start.99 = (bf16[256,1024]{1,0:T(8,128)(2,1)}, bf16[256,1024]{1,0:T(8,128)(2,1)S(1)}, u32[]{:S(2)}, u32[]{:S(2)}) collective-permute-start(bf16[256,1024]{1,0:T(8,128)(2,1)} %get-tuple-element.383), channel_id=1, source_target_pairs={{0,3},{1,0},{2,1},{3,2},{4,7},{5,4},{6,5},{7,6},{8,11},{9,8},{10,9... | collective-permute-start | bytes 1572872 | tf_op jit(solution)/shard_map/ppermute | solution.py:28
  71.0 6.4 %collective-permute-start.106 = (bf16[224,256]{1,0:T(8,128)(2,1)S(1)}, bf16[224,256]{1,0:T(8,128)(2,1)S(1)}, u32[]{:S(2)}, u32[]{:S(2)}) collective-permute-start(bf16[224,256]{1,0:T(8,128)(2,1)S(1)} %get-tuple-element.392), channel_id=1, source_target_pairs={{0,1},{1,2},{2,3},{3,0},{4,5},{5,6},{6,7},{7,4},{8,9},{9,10},{10,1... | collective-permute-start | bytes 344072 | tf_op jit(solution)/shard_map/ppermute | solution.py:28
  73.5 9.9 %collective-permute-start.107 = (bf16[224,256]{1,0:T(8,128)(2,1)S(1)}, bf16[224,256]{1,0:T(8,128)(2,1)S(1)}, u32[]{:S(2)}, u32[]{:S(2)}) collective-permute-start(bf16[224,256]{1,0:T(8,128)(2,1)S(1)} %get-tuple-element.393), channel_id=1, source_target_pairs={{0,2},{1,3},{2,0},{3,1},{4,6},{5,7},{6,4},{7,5},{8,10},{9,11},{10,... | collective-permute-start | bytes 344072 | tf_op jit(solution)/shard_map/ppermute | solution.py:28
  74.6 8.8 %collective-permute-start.108 = (bf16[224,256]{1,0:T(8,128)(2,1)S(1)}, bf16[224,256]{1,0:T(8,128)(2,1)S(1)}, u32[]{:S(2)}, u32[]{:S(2)}) collective-permute-start(bf16[224,256]{1,0:T(8,128)(2,1)S(1)} %get-tuple-element.394), channel_id=1, source_target_pairs={{0,3},{1,0},{2,1},{3,2},{4,7},{5,4},{6,5},{7,6},{8,11},{9,8},{10,9... | collective-permute-start | bytes 344072 | tf_op jit(solution)/shard_map/ppermute | solution.py:28
  76.9 15.3 %collective-permute-start.100 = (bf16[224,256]{1,0:T(8,128)(2,1)S(1)}, bf16[224,256]{1,0:T(8,128)(2,1)S(1)}, u32[]{:S(2)}, u32[]{:S(2)}) collective-permute-start(bf16[224,256]{1,0:T(8,128)(2,1)S(1)} %get-tuple-element.387), channel_id=1, source_target_pairs={{0,1},{1,2},{2,3},{3,0},{4,5},{5,6},{6,7},{7,4},{8,9},{9,10},{10,1... | collective-permute-start | bytes 344072 | tf_op jit(solution)/shard_map/ppermute | solution.py:28
  76.9 16.2 %collective-permute-start.101 = (bf16[224,256]{1,0:T(8,128)(2,1)S(1)}, bf16[224,256]{1,0:T(8,128)(2,1)S(1)}, u32[]{:S(2)}, u32[]{:S(2)}) collective-permute-start(bf16[224,256]{1,0:T(8,128)(2,1)S(1)} %get-tuple-element.388), channel_id=1, source_target_pairs={{0,2},{1,3},{2,0},{3,1},{4,6},{5,7},{6,4},{7,5},{8,10},{9,11},{10,... | collective-permute-start | bytes 344072 | tf_op jit(solution)/shard_map/ppermute | solution.py:28
  77.4 15.7 %collective-permute-start.102 = (bf16[224,256]{1,0:T(8,128)(2,1)S(1)}, bf16[224,256]{1,0:T(8,128)(2,1)S(1)}, u32[]{:S(2)}, u32[]{:S(2)}) collective-permute-start(bf16[224,256]{1,0:T(8,128)(2,1)S(1)} %get-tuple-element.389), channel_id=1, source_target_pairs={{0,3},{1,0},{2,1},{3,2},{4,7},{5,4},{6,5},{7,6},{8,11},{9,8},{10,9... | collective-permute-start | bytes 344072 | tf_op jit(solution)/shard_map/ppermute | solution.py:28
  83.5 15.6 %collective-permute-start.111 = (bf16[224,256]{1,0:T(8,128)(2,1)S(1)}, bf16[224,256]{1,0:T(8,128)(2,1)S(1)}, u32[]{:S(2)}, u32[]{:S(2)}) collective-permute-start(bf16[224,256]{1,0:T(8,128)(2,1)S(1)} %add_convert_fusion.refs_0_), channel_id=1, source_target_pairs={{0,3},{1,0},{2,1},{3,2},{4,7},{5,4},{6,5},{7,6},{8,11},{9,8},{10,9... | collective-permute-start | bytes 344072 | tf_op jit(solution)/shard_map/ppermute | solution.py:28
  91.6 9.2 %collective-permute-start.110 = (bf16[224,256]{1,0:T(8,128)(2,1)S(1)}, bf16[224,256]{1,0:T(8,128)(2,1)S(1)}, u32[]{:S(2)}, u32[]{:S(2)}) collective-permute-start(bf16[224,256]{1,0:T(8,128)(2,1)S(1)} %add_convert_fusion.refs_0_), channel_id=1, source_target_pairs={{0,2},{1,3},{2,0},{3,1},{4,6},{5,7},{6,4},{7,5},{8,10},{9,11},{10,... | collective-permute-start | bytes 344072 | tf_op jit(solution)/shard_map/ppermute | solution.py:28
  92.2 8.6 %collective-permute-start.109 = (bf16[224,256]{1,0:T(8,128)(2,1)S(1)}, bf16[224,256]{1,0:T(8,128)(2,1)S(1)}, u32[]{:S(2)}, u32[]{:S(2)}) collective-permute-start(bf16[224,256]{1,0:T(8,128)(2,1)S(1)} %add_convert_fusion.refs_0_), channel_id=1, source_target_pairs={{0,1},{1,2},{2,3},{3,0},{4,5},{5,6},{6,7},{7,4},{8,9},{9,10},{10,1... | collective-permute-start | bytes 344072 | tf_op jit(solution)/shard_map/ppermute | solution.py:28
  93.2 9.0 %collective-permute-start.105 = (bf16[224,256]{1,0:T(8,128)(2,1)S(1)}, bf16[224,256]{1,0:T(8,128)(2,1)S(1)}, u32[]{:S(2)}, u32[]{:S(2)}) collective-permute-start(bf16[224,256]{1,0:T(8,128)(2,1)S(1)} %add_convert_fusion.1.refs_0_), channel_id=1, source_target_pairs={{0,3},{1,0},{2,1},{3,2},{4,7},{5,4},{6,5},{7,6},{8,11},{9,8},{10,9... | collective-permute-start | bytes 344072 | tf_op jit(solution)/shard_map/ppermute | solution.py:28
  99.1 5.9 %collective-permute-start.104 = (bf16[224,256]{1,0:T(8,128)(2,1)S(1)}, bf16[224,256]{1,0:T(8,128)(2,1)S(1)}, u32[]{:S(2)}, u32[]{:S(2)}) collective-permute-start(bf16[224,256]{1,0:T(8,128)(2,1)S(1)} %add_convert_fusion.1.refs_0_), channel_id=1, source_target_pairs={{0,2},{1,3},{2,0},{3,1},{4,6},{5,7},{6,4},{7,5},{8,10},{9,11},{10,... | collective-permute-start | bytes 344072 | tf_op jit(solution)/shard_map/ppermute | solution.py:28
  99.1 5.9 %collective-permute-start.103 = (bf16[224,256]{1,0:T(8,128)(2,1)S(1)}, bf16[224,256]{1,0:T(8,128)(2,1)S(1)}, u32[]{:S(2)}, u32[]{:S(2)}) collective-permute-start(bf16[224,256]{1,0:T(8,128)(2,1)S(1)} %add_convert_fusion.1.refs_0_), channel_id=1, source_target_pairs={{0,1},{1,2},{2,3},{3,0},{4,5},{5,6},{6,7},{7,4},{8,9},{9,10},{10,1... | collective-permute-start | bytes 344072 | tf_op jit(solution)/shard_map/ppermute | solution.py:28
  102.1 13.0 %collective-permute-start.117 = (bf16[1024,256]{1,0:T(8,128)(2,1)S(1)}, bf16[1024,256]{1,0:T(8,128)(2,1)S(1)}, u32[]{:S(2)}, u32[]{:S(2)}) collective-permute-start(bf16[1024,256]{1,0:T(8,128)(2,1)S(1)} %get-tuple-element.400), channel_id=1, source_target_pairs={{0,4},{4,0},{8,12},{12,8},{16,20},{20,16},{24,28},{28,24},{1,5},{5... | collective-permute-start | bytes 1572872 | tf_op jit(solution)/shard_map/ppermute | solution.py:22
  106.2 8.8 %collective-permute-start.116 = (bf16[1024,256]{1,0:T(8,128)(2,1)S(1)}, bf16[1024,256]{1,0:T(8,128)(2,1)S(1)}, u32[]{:S(2)}, u32[]{:S(2)}) collective-permute-start(bf16[1024,256]{1,0:T(8,128)(2,1)S(1)} %get-tuple-element.399), channel_id=1, source_target_pairs={{0,4},{4,0},{8,12},{12,8},{16,20},{20,16},{24,28},{28,24},{1,5},{5... | collective-permute-start | bytes 1572872 | tf_op jit(solution)/shard_map/ppermute | solution.py:22
  106.3 3.1 %collective-permute-start.114 = (f32[8,128]{1,0:T(8,128)S(1)}, f32[8,128]{1,0:T(8,128)S(1)}, u32[]{:S(2)}, u32[]{:S(2)}) collective-permute-start(f32[8,128]{1,0:T(8,128)S(1)} %add.284), channel_id=1, source_target_pairs={{0,3},{1,0},{2,1},{3,2},{4,7},{5,4},{6,5},{7,6},{8,11},{9,8},{10,9... | collective-permute-start | bytes 12296 | tf_op jit(solution)/shard_map/ppermute | solution.py:28
  107.6 3.4 %collective-permute-start.113 = (f32[8,128]{1,0:T(8,128)S(1)}, f32[8,128]{1,0:T(8,128)S(1)}, u32[]{:S(2)}, u32[]{:S(2)}) collective-permute-start(f32[8,128]{1,0:T(8,128)S(1)} %add.284), channel_id=1, source_target_pairs={{0,2},{1,3},{2,0},{3,1},{4,6},{5,7},{6,4},{7,5},{8,10},{9,11},{10,... | collective-permute-start | bytes 12296 | tf_op jit(solution)/shard_map/ppermute | solution.py:28
  108.0 4.3 %collective-permute-start.112 = (f32[8,128]{1,0:T(8,128)S(1)}, f32[8,128]{1,0:T(8,128)S(1)}, u32[]{:S(2)}, u32[]{:S(2)}) collective-permute-start(f32[8,128]{1,0:T(8,128)S(1)} %add.284), channel_id=1, source_target_pairs={{0,1},{1,2},{2,3},{3,0},{4,5},{5,6},{6,7},{7,4},{8,9},{9,10},{10,1... | collective-permute-start | bytes 12296 | tf_op jit(solution)/shard_map/ppermute | solution.py:28
  112.3 2.8 %collective-permute-start.115 = (f32[8,128]{1,0:T(8,128)S(1)}, f32[8,128]{1,0:T(8,128)S(1)}, u32[]{:S(2)}, u32[]{:S(2)}) collective-permute-start(f32[8,128]{1,0:T(8,128)S(1)} %add_add_fusion.32.own_ref), channel_id=1, source_target_pairs={{0,4},{4,0},{8,12},{12,8},{16,20},{20,16},{24,28},{28,24},{1,5},{5... | collective-permute-start | bytes 12296 | tf_op jit(solution)/shard_map/ppermute | solution.py:22
  (4 other events, 3.6 us)
